TPU v7x, 32 devices: a whole 2x2x4 slice. The times are simulated.
32 devices in a mesh: dom: 8 (over z, x), cls: 4 (over y, core).
Axes of the slice: x: 2, y: 2, z: 4, core: 2. Of those that a mesh axis runs over, the one named last changes fastest.
Arguments:
- particles: bfloat16 [256, 16384], P(('dom', 'cls')), may hold values from -6 to 6
- references: bfloat16 [64, 16384], P('cls'), may hold values from -0.046875 to 0.046875
- pose_weights: int32 [256, 24, 64], P(('dom', 'cls')), may hold values from 0 to 4
- class_mask: int32 [256, 64], P(('dom', 'cls')), may hold values 0 or 1
Outputs:
- class_scores: float32 [256, 64], P(('dom', 'cls'))
- class_sums: float32 [64, 16384], P('cls', 'dom')
All inputs are finite; a program needn't handle non-finite values. No bound on the sum of `class_mask` on one device may be relied on, other than what follows from the above.
Results may differ from a plain program's by a relative error of at most 0.0003.
Values may be sent and summed in bfloat16 or wider, within the bound.
No kernel may reach another device: no remote copies, remote signals or barrier semaphores. Data moves between devices by JAX's collectives and lax.ppermute only.
A program may use at most 128 MiB of HBM per device.

v0:
```python
import math
import jax
import jax.numpy as jnp
from jax import lax
from jax.sharding import PartitionSpec as P

CYCLES = 64
ANG = 256
ROT = 24


def turned(images, shift_by):
    shape_in = images.shape
    polar = images.reshape(shape_in[:-1] + (CYCLES, ANG))
    return jnp.roll(polar, shift_by, axis=-1).reshape(shape_in)


def on_device(particles, references, pose_weights, class_mask):
    n_rows = particles.shape[0]
    angle_step = ANG // ROT
    weights = pose_weights * class_mask[:, None, :]
    weights_f = weights.astype(jnp.float32)
    weights_b = weights.astype(jnp.bfloat16)
    rotated = jnp.stack([turned(particles, -r * angle_step) for r in range(ROT)], axis=0)
    rotated_rows = rotated.reshape(ROT * n_rows, rotated.shape[2])
    ref_piece = lax.all_gather(references, "cls", axis=0, tiled=True)
    width_now = ref_piece.shape[0]
    corr = jnp.dot(rotated_rows, ref_piece.T, preferred_element_type=jnp.float32)
    corr = corr.reshape(ROT, n_rows, width_now)
    weight_cols = weights_f
    scored = jnp.einsum("rnk,nrk->nk", corr, weight_cols) / ROT
    weight_cols = weights_b
    local_sums = lax.psum_scatter(
        jnp.einsum("nrk,rnl->kl", weight_cols, rotated, preferred_element_type=jnp.float32),
        "cls",
        scatter_dimension=0,
        tiled=True,
    )
    home_part = lax.psum_scatter(local_sums, "dom", scatter_dimension=1, tiled=True)
    particle_total = n_rows * lax.axis_size("dom") * lax.axis_size("cls")
    class_sums = home_part / math.sqrt(particle_total * ROT)
    return (scored, class_sums)


def solution(mesh):
    return jax.shard_map(
        on_device,
        mesh=mesh,
        in_specs=(
            P(("dom", "cls"), None),
            P("cls", None),
            P(("dom", "cls"), None, None),
            P(("dom", "cls"), None),
        ),
        out_specs=(P(("dom", "cls"), None), P("cls", "dom")),
        check_vma=False,
    )
```

profile of v0, /device:TPU:0, one launch (start us, length us, event | category | flops | bytes accessed | tf_op | source)
XLA Modules:
  0.0 300.9 jit_solution(10851470049415356779)
XLA Ops:
  7.2 1.1 slice.238
  16.4 1.6 slice.247
  19.1 1.6 slice.249
  20.6 1.8 slice.250
  22.5 1.6 slice.251
  24.0 1.8 slice.252
  25.8 1.6 slice.253
  49.3 1.8 stack_reshape.106
  53.8 1.8 stack_reshape.107
  58.3 1.7 stack_reshape.96
  62.8 1.8 stack_reshape.97
  67.3 1.8 stack_reshape.98
  71.8 1.8 stack_reshape.99
  75.4 1.7 stack_reshape.108
  79.0 1.7 stack_reshape.109
  82.6 1.8 stack_reshape.110
  86.2 1.8 stack_reshape.111
  89.7 1.7 stack_reshape.112
  93.3 1.7 stack_reshape.113
  96.9 1.8 stack_reshape.114
  100.5 1.8 stack_reshape.115
  104.1 1.7 stack_reshape.116
  107.7 1.7 stack_reshape.117
  110.3 1.8 stack_reshape.118
  112.1 1.2 copy.98
  113.3 34.4 %stack.3 = bf16[24,8,16384]{2,0,1:T(8,128)(2,1)} concatenate(bf16[1,8,16384]{2,0,1:T(2,128)(2,1)} %copy.98, bf16[1,8,16384]{2,0,1:T(2,128)(2,1)} %stack_reshape.96, bf16[1,8,16384]{2,0,1:T(2,128)(2,1)} %stack_reshape.97, bf16[1,8,16384]{2,0,1:T(2,128)(2,1)} %stack_reshape.98, bf16[1,8,16384]{2,0,1:T(2,128)(2,1)} %stack_reshape.99, bf16[1,8,16384]{2,0,1:T(2,128)(2,1)S(1)} %stack_reshape.100, ...), dimensions={0} | concatenate | bytes 12582912 | tf_op jit(solution)/shard_map/stack | solution.py:24
  147.7 6.2 %convolution_bitcast_fusion = f32[64,16384]{1,0:T(8,128)} fusion(bf16[24,8,16384]{2,0,1:T(8,128)(2,1)} %stack.3, s32[8,24,64]{2,1,0:T(8,128)S(1)} %copy-done.2, s32[8,64]{1,0:T(8,128)S(1)} %copy-done.1), kind=kOutput, calls=%fused_computation | convolution fusion | flops 402677760 | bytes 10536960 | tf_op jit(solution)/shard_map/nrk,rnl->kl/dot_general | solution.py:34
  154.7 46.6 %reduce-scatter.3.cloned.1.call-done = f32[16,16384]{1,0:T(8,128)} async-done(((f32[64,16384]{1,0:T(8,128)}), f32[16,16384]{1,0:T(8,128)}) %reduce-scatter.3.cloned.1.call-update) | async-done | bytes 1048592 | tf_op jit(solution)/shard_map/reduce_scatter | solution.py:33
  201.3 24.2 %all-gather.2.cloned.1.call-done = bf16[64,16384]{1,0:T(8,128)(2,1)} async-done(((bf16[16,16384]{1,0:T(8,128)(2,1)}), bf16[64,16384]{1,0:T(8,128)(2,1)}) %all-gather.2.cloned.1.call-update) | async-done | bytes 2097168 | tf_op jit(solution)/shard_map/all_gather | solution.py:26
  225.5 5.2 %fusion.8 = f32[8,64]{1,0:T(8,128)S(1)} fusion(bf16[24,8,16384]{2,0,1:T(8,128)(2,1)} %stack.3, bf16[64,16384]{1,0:T(8,128)(2,1)} %all-gather.2.cloned.1.call-done, s32[8,24,64]{2,1,0:T(8,128)S(1)} %copy-done.2, s32[8,64]{1,0:T(8,128)S(1)} %copy-done.1), kind=kOutput, calls=%fused_computation.5 | convolution fusion | flops 402701824 | bytes 8441856 | tf_op jit(solution)/shard_map/dot_general | solution.py:28
  231.3 61.4 %reduce-scatter.5.cloned.1.call-done = f32[16,2048]{1,0:T(8,128)} async-done(((f32[16,16384]{1,0:T(8,128)}), f32[16,2048]{1,0:T(8,128)}) %reduce-scatter.5.cloned.1.call-update) | async-done | bytes 131088 | tf_op jit(solution)/shard_map/reduce_scatter | solution.py:39
  292.8 1.6 broadcast_multiply_fusion
  (116 shorter events, 65.0 us)
Async XLA Ops:
  7.2 20.2 %copy-start = (bf16[8,16384]{1,0:T(8,128)(2,1)S(1)}, bf16[8,16384]{1,0:T(8,128)(2,1)}, u32[]{:S(2)}) copy-start(bf16[8,16384]{1,0:T(8,128)(2,1)} %param.4) | copy-start | bytes 786436
  7.2 194.1 %reduce-scatter.3.cloned.1.call-start = ((), (), s32[]{:S(2)}) async-start(), calls=%async_computation.3 | async-start | bytes 5242880 | tf_op jit(solution)/shard_map/reduce_scatter | solution.py:33
  113.3 34.4 %copy-start.1 = (s32[8,64]{1,0:T(8,128)S(1)}, s32[8,64]{1,0:T(8,128)}, u32[]{:S(2)}) copy-start(s32[8,64]{1,0:T(8,128)} %param.7) | copy-start | bytes 6148
  113.3 34.4 %copy-start.2 = (s32[8,24,64]{2,1,0:T(8,128)S(1)}, s32[8,24,64]{2,1,0:T(8,128)}, u32[]{:S(2)}) copy-start(s32[8,24,64]{2,1,0:T(8,128)} %param.6) | copy-start | bytes 147460
  153.9 71.6 %all-gather.2.cloned.1.call-start = ((), (), s32[]{:S(2)}) async-start(), calls=%async_computation.2 | async-start | bytes 2621440 | tf_op jit(solution)/shard_map/all_gather | solution.py:26
  154.6 138.1 %reduce-scatter.5.cloned.1.call-start = ((), (), s32[]{:S(2)}) async-start(), calls=%async_computation.4 | async-start | bytes 1179648 | tf_op jit(solution)/shard_map/reduce_scatter | solution.py:39
Sparse Core Ops, SparseCore 0:
  154.0 47.2 reduce-scatter.2
  202.9 22.5 all-gather.1
  229.3 63.4 reduce-scatter.4
where the time goes:
time: 306 us; the launch traced here: 301 us
  waiting for transfers between devices  133 us (43%)
  local copies, waits for them, and re-layouts  125 us (41%)
  other arithmetic  17.7 us (6%)
  between operations  14.2 us (5%)
  matrix products  11.4 us (4%)
    another operation x25, local copies, waits for them, and re-layouts, on_device(): jnp.stack([turned(particles, -r * angle_step) for r in range(ROT)], axis=0)  67.3 us
    reduce_scatter x1, waiting for transfers between devices, on_device(): lax.psum_scatter(local_sums, 'dom', scatter_dimension=1, tiled=True)  61.4 us
    reduce_scatter x1, waiting for transfers between devices, on_device(): lax.psum_scatter(jnp.einsum('nrk,rnl->kl', weight_cols, rotated, preferre...  46.6 us
    slice x35, local copies, waits for them, and re-layouts, turned(): return jnp.roll(polar, shift_by, axis=-1).reshape(shape_in)  33.7 us
    all_gather x1, waiting for transfers between devices, on_device(): ref_piece = lax.all_gather(references, 'cls', axis=0, tiled=True)  24.2 us
    unnamed x52, local copies, waits for them, and re-layouts  23.6 us
    concatenate x23, other arithmetic, turned(): return jnp.roll(polar, shift_by, axis=-1).reshape(shape_in)  15.5 us
    dot_general x1, matrix products, on_device(): jnp.einsum('nrk,rnl->kl', weight_cols, rotated, preferred_element_type=jn...  6.15 us
  transfers between devices with their start and end apart: 3, of which 3 were waited for; matrix products, arithmetic and copies ran while one was open for 2% of the time, Pallas kernels for 0%

commit v1 on v0

--- a/solution.py
+++ b/solution.py
@@ -3,10 +3,33 @@
 import jax.numpy as jnp
 from jax import lax
 from jax.sharding import PartitionSpec as P
+from jax.lax import axis_index, axis_size, ppermute
 
 CYCLES = 64
 ANG = 256
 ROT = 24
+
+
+def lanes_derive(arr, dim_i):
+    arr = jnp.moveaxis(arr, 0, dim_i)
+    after = arr.shape
+    a_now = arr.reshape(*after[:dim_i], after[dim_i] * after[dim_i + 1], *after[dim_i + 2 :])
+    return a_now
+
+
+def axis_part_work(arr_in, which_axis):
+    oldest, x_new = (axis_size(which_axis), axis_index(which_axis))
+    tile_out, g_now = (arr_in[None], 1)
+    while g_now < oldest:
+        long_array = ppermute(
+            tile_out, which_axis, perm=tuple(((rr, rr ^ g_now) for rr in range(oldest)))
+        )
+        u1 = x_new & g_now == 0
+        tile_out = jnp.concatenate(
+            [jnp.where(u1, tile_out, long_array), jnp.where(u1, long_array, tile_out)]
+        )
+        g_now *= 2
+    return tile_out
 
 
 def turned(images, shift_by):
@@ -23,7 +46,7 @@
     weights_b = weights.astype(jnp.bfloat16)
     rotated = jnp.stack([turned(particles, -r * angle_step) for r in range(ROT)], axis=0)
     rotated_rows = rotated.reshape(ROT * n_rows, rotated.shape[2])
-    ref_piece = lax.all_gather(references, "cls", axis=0, tiled=True)
+    ref_piece = lanes_derive(axis_part_work(references, "cls"), 0)
     width_now = ref_piece.shape[0]
     corr = jnp.dot(rotated_rows, ref_piece.T, preferred_element_type=jnp.float32)
     corr = corr.reshape(ROT, n_rows, width_now)

time: 306 us -> 285 us (0.931)
  waiting for transfers between devices: 133 us -> 110 us
  local copies, waits for them, and re-layouts: 125 us -> 121 us
  starting transfers between devices: 0.12 us -> 3.38 us
    reduce_scatter x1, waiting for transfers between devices: 46.6 us -> 16 us  [on_device(): lax.psum_scatter(jnp.einsum('nrk,rnl->kl', weight_cols, rotated, preferre...]
    ppermute x0 -> x2, waiting for transfers between devices: none -> 30.3 us  [axis_part_work(): ppermute(tile_out, which_axis, perm=tuple(((rr, rr ^ g_now) for rr in ran...]
    all_gather x1 -> x0, waiting for transfers between devices: 24.2 us -> none  [on_device(): ref_piece = lax.all_gather(references, 'cls', axis=0, tiled=True)]
    slice x35, local copies, waits for them, and re-layouts: 33.7 us -> 29.2 us  [turned(): return jnp.roll(polar, shift_by, axis=-1).reshape(shape_in)]
    ppermute x0 -> x2, starting transfers between devices: none -> 3.12 us  [axis_part_work(): ppermute(tile_out, which_axis, perm=tuple(((rr, rr ^ g_now) for rr in ran...]
    unnamed x52 -> x54, local copies, waits for them, and re-layouts: 23.6 us -> 24.3 us
  transfers between devices with their start and end apart: 3 -> 4, of which waited for: 3 -> 3; matrix products, arithmetic and copies ran while one was open for 2% -> 54% of each run, Pallas kernels for 0% -> 0%
where the time goes in v1:
time: 285 us; the launch traced here: 280 us
  local copies, waits for them, and re-layouts  121 us (42%)
  waiting for transfers between devices  110 us (39%)
  other arithmetic  20.6 us (7%)
  between operations  14.5 us (5%)
  matrix products  10.8 us (4%)
  starting transfers between devices  3.38 us (1%)
    another operation x25, local copies, waits for them, and re-layouts, on_device(): jnp.stack([turned(particles, -r * angle_step) for r in range(ROT)], axis=0)  67.2 us
    reduce_scatter x1, waiting for transfers between devices, on_device(): lax.psum_scatter(local_sums, 'dom', scatter_dimension=1, tiled=True)  63.3 us
    ppermute x2, waiting for transfers between devices, axis_part_work(): ppermute(tile_out, which_axis, perm=tuple(((rr, rr ^ g_now) for rr in ran...  30.3 us
    slice x35, local copies, waits for them, and re-layouts, turned(): return jnp.roll(polar, shift_by, axis=-1).reshape(shape_in)  29.2 us
    unnamed x54, local copies, waits for them, and re-layouts  24.3 us
    reduce_scatter x1, waiting for transfers between devices, on_device(): lax.psum_scatter(jnp.einsum('nrk,rnl->kl', weight_cols, rotated, preferre...  16 us
    concatenate x23, other arithmetic, turned(): return jnp.roll(polar, shift_by, axis=-1).reshape(shape_in)  15.6 us
    dot_general x1, matrix products, on_device(): jnp.einsum('nrk,rnl->kl', weight_cols, rotated, preferred_element_type=jn...  6.16 us
  transfers between devices with their start and end apart: 4, of which 3 were waited for; matrix products, arithmetic and copies ran while one was open for 54% of the time, Pallas kernels for 0%

profile of v1, /device:TPU:0, one launch (start us, length us, event | category | flops | bytes accessed | tf_op | source)
XLA Modules:
  0.0 279.7 jit_solution(933967110644012055)
XLA Ops:
  9.8 1.1 slice.240
  11.8 1.1 slice.242
  15.8 1.1 slice.246
  16.9 1.6 slice.247
  45.3 1.8 stack_reshape.106
  49.8 1.8 stack_reshape.107
  54.3 1.7 stack_reshape.96
  58.7 1.8 stack_reshape.97
  63.3 1.8 stack_reshape.98
  67.8 1.8 stack_reshape.99
  71.5 1.7 stack_reshape.108
  75.0 1.7 stack_reshape.109
  78.6 1.8 stack_reshape.110
  82.2 1.8 stack_reshape.111
  85.8 1.8 stack_reshape.112
  89.4 1.8 stack_reshape.113
  93.0 1.8 stack_reshape.114
  96.6 1.7 stack_reshape.115
  100.2 1.7 stack_reshape.116
  103.8 1.8 stack_reshape.117
  106.5 1.8 stack_reshape.118
  108.2 1.2 copy.98
  109.4 34.4 %stack.3 = bf16[24,8,16384]{2,0,1:T(8,128)(2,1)} concatenate(bf16[1,8,16384]{2,0,1:T(2,128)(2,1)} %copy.98, bf16[1,8,16384]{2,0,1:T(2,128)(2,1)} %stack_reshape.96, bf16[1,8,16384]{2,0,1:T(2,128)(2,1)} %stack_reshape.97, bf16[1,8,16384]{2,0,1:T(2,128)(2,1)} %stack_reshape.98, bf16[1,8,16384]{2,0,1:T(2,128)(2,1)} %stack_reshape.99, bf16[1,8,16384]{2,0,1:T(2,128)(2,1)S(1)} %stack_reshape.100, ...), dimensions={0} | concatenate | bytes 12582912 | tf_op jit(solution)/shard_map/stack | solution.py:47
  143.8 6.2 %convolution_bitcast_fusion = f32[64,16384]{1,0:T(8,128)} fusion(bf16[24,8,16384]{2,0,1:T(8,128)(2,1)} %stack.3, s32[8,24,64]{2,1,0:T(8,128)S(1)} %copy-done.3, s32[8,64]{1,0:T(8,128)S(1)} %copy-done.2), kind=kOutput, calls=%fused_computation | convolution fusion | flops 402677760 | bytes 10536960 | tf_op jit(solution)/shard_map/nrk,rnl->kl/dot_general | solution.py:57
  151.0 1.1 broadcast_select_fusion.3
  152.2 2.6 collective-permute-start.1
  154.8 30.3 %collective-permute-done.1 = bf16[2,16,16384]{2,1,0:T(8,128)(2,1)} collective-permute-done((bf16[2,16,16384]{2,1,0:T(8,128)(2,1)S(1)}, bf16[2,16,16384]{2,1,0:T(8,128)(2,1)}, u32[]{:S(2)}, u32[]{:S(2)}) %collective-permute-start.1) | collective-permute-done | bytes 1048608 | tf_op jit(solution)/shard_map/ppermute | solution.py:24
  185.1 1.4 broadcast_select_fusion.1
  186.5 16.0 %reduce-scatter.3.cloned.1.call-done = f32[16,16384]{1,0:T(8,128)} async-done(((f32[64,16384]{1,0:T(8,128)}), f32[16,16384]{1,0:T(8,128)}) %reduce-scatter.3.cloned.1.call-update) | async-done | bytes 1048592 | tf_op jit(solution)/shard_map/reduce_scatter | solution.py:56
  202.7 4.6 %fusion.1 = f32[8,64]{1,0:T(8,128)S(1)} fusion(bf16[24,8,16384]{2,0,1:T(8,128)(2,1)} %stack.3, bf16[64,16384,1]{1,0,2:T(8,128)(2,1)S(1)} %bitcast.80, s32[8,24,64]{2,1,0:T(8,128)S(1)} %copy-done.3, s32[8,64]{1,0:T(8,128)S(1)} %copy-done.2), kind=kOutput, calls=%fused_computation.4 | convolution fusion | flops 402701824 | bytes 8441856 | tf_op jit(solution)/shard_map/dot_general | solution.py:51
  208.0 63.3 %reduce-scatter.5.cloned.1.call-done = f32[16,2048]{1,0:T(8,128)} async-done(((f32[16,16384]{1,0:T(8,128)}), f32[16,2048]{1,0:T(8,128)}) %reduce-scatter.5.cloned.1.call-update) | async-done | bytes 131088 | tf_op jit(solution)/shard_map/reduce_scatter | solution.py:62
  271.3 1.6 broadcast_multiply_fusion
  (123 shorter events, 67.8 us)
Async XLA Ops:
  7.2 12.4 %copy-start = (bf16[8,16384]{1,0:T(8,128)(2,1)S(1)}, bf16[8,16384]{1,0:T(8,128)(2,1)}, u32[]{:S(2)}) copy-start(bf16[8,16384]{1,0:T(8,128)(2,1)} %param.4) | copy-start | bytes 786436
  7.2 195.3 %reduce-scatter.3.cloned.1.call-start = ((), (), s32[]{:S(2)}) async-start(), calls=%async_computation.2 | async-start | bytes 5242880 | tf_op jit(solution)/shard_map/reduce_scatter | solution.py:56
  7.2 143.0 %collective-permute-start = (bf16[1,16,16384]{2,1,0:T(8,128)(2,1)}, bf16[1,16,16384]{2,1,0:T(8,128)(2,1)}, u32[]{:S(2)}, u32[]{:S(2)}) collective-permute-start(bf16[1,16,16384]{2,1,0:T(8,128)(2,1)} %bitcast.81), channel_id=1, source_target_pairs={{0,1},{1,0},{2,3},{3,2},{4,5},{5,4},{6,7},{7,6},{8,9},{9,8},{10,11... | collective-permute-start | bytes 1572872 | tf_op jit(solution)/shard_map/ppermute | solution.py:24
  109.4 34.4 %copy-start.2 = (s32[8,64]{1,0:T(8,128)S(1)}, s32[8,64]{1,0:T(8,128)}, u32[]{:S(2)}) copy-start(s32[8,64]{1,0:T(8,128)} %param.7) | copy-start | bytes 6148
  109.4 34.4 %copy-start.3 = (s32[8,24,64]{2,1,0:T(8,128)S(1)}, s32[8,24,64]{2,1,0:T(8,128)}, u32[]{:S(2)}) copy-start(s32[8,24,64]{2,1,0:T(8,128)} %param.6) | copy-start | bytes 147460
  150.0 1.0 copy-start.1
  150.0 121.3 %reduce-scatter.5.cloned.1.call-start = ((), (), s32[]{:S(2)}) async-start(), calls=%async_computation.3 | async-start | bytes 1179648 | tf_op jit(solution)/shard_map/reduce_scatter | solution.py:62
  152.2 32.9 %collective-permute-start.1 = (bf16[2,16,16384]{2,1,0:T(8,128)(2,1)S(1)}, bf16[2,16,16384]{2,1,0:T(8,128)(2,1)}, u32[]{:S(2)}, u32[]{:S(2)}) collective-permute-start(bf16[2,16,16384]{2,1,0:T(8,128)(2,1)S(1)} %pad_maximum_fusion.1), channel_id=1, source_target_pairs={{0,2},{1,3},{2,0},{3,1},{4,6},{5,7},{6,4},{7,5},{8,10},{9,11},{10,... | collective-permute-start | bytes 3145736 | tf_op jit(solution)/shard_map/ppermute | solution.py:24
Sparse Core Ops, SparseCore 0:
  150.1 52.3 reduce-scatter.2
  206.3 64.9 reduce-scatter.4
